TPU v7x, 32 devices: a whole 2x2x4 slice. The times are simulated.
32 devices in a mesh: sy: 16 (over z, y, x), sx: 2 (over core).
Axes of the slice: x: 2, y: 2, z: 4, core: 2. Of those that a mesh axis runs over, the one named last changes fastest.
Arguments:
- object_slices: bfloat16 [2, 2, 2048, 2048], P(None, None, 'sy', 'sx'), may hold values from -4 to 4
- probe_wave: float32 [2, 256, 256], replicated, may hold values from -4 to 4
- propagator_phase: float32 [256, 256], replicated, may hold values from -3.140625 to 3.140625
- intensities: bfloat16 [16, 2, 4, 256, 256], P('sy', 'sx'), may hold values from 0 to 2
- scan_offsets: int32 [16, 2, 4, 2], P('sy', 'sx'), may hold values from 0 to 1023, as said below
- live_counts: int32 [16, 2], P('sy', 'sx'), may hold values from 1 to 4, as said below
Outputs:
- object_gradient: float32 [2, 2, 2048, 2048], P(None, None, 'sy', 'sx')
- probe_gradient: float32 [2, 256, 256], replicated
Inputs may be any that keep to these rules, and one draw needn't show every extreme that they name: `scan_offsets`: row offsets lie in 0 to 127 and column offsets in 0 to 1023. The first live_counts[u, v] slots of tile (u, v) are live, the rest are not.
All inputs are finite; a program needn't handle non-finite values.
Results may differ from a plain program's by a relative error of at most 0.0004.
Values may be sent and summed in bfloat16 or wider, within the bound.
A program may use at most 128 MiB of HBM per device.

v0:
```python
import math

import jax
import jax.numpy as jnp
from jax import lax
from jax.sharding import PartitionSpec as P


def passed_along(block, axis, distance):
    devices = range(lax.axis_size(axis))
    route = [(i - distance, i) for i in devices if i - distance in devices]
    return lax.ppermute(block, axis, route)


def with_halo(cells, sides, width):
    for axis, dim in sides:
        count = lax.axis_size(axis)
        ends = count - 1
        head = lax.slice_in_dim(cells, 0, width, axis=dim)
        tail = lax.slice_in_dim(cells, cells.shape[dim] - width, cells.shape[dim], axis=dim)
        cells = jnp.concatenate(
            [
                lax.ppermute(tail, axis, [(i, (i + 1) % count) for i in range(ends)]),
                cells,
                lax.ppermute(head, axis, [((i + 1) % count, i) for i in range(ends)]),
            ],
            axis=dim,
        )
    return cells


def precise_dot(left, right):
    return jnp.dot(left, right, precision=lax.Precision.HIGHEST, preferred_element_type=jnp.float32)


def dft_tables(window):
    steps = jnp.arange(window, dtype=jnp.int32)
    products = steps[:, None] * steps[None, :] % window
    phases = -2.0 * math.pi / window * products.astype(jnp.float32)
    factor = 1.0 / math.sqrt(window)
    return (jnp.cos(phases) * factor, jnp.sin(phases) * factor)


def transform(value_re, value_im, cos_table, sin_table):
    left_re = precise_dot(cos_table, value_re) - precise_dot(sin_table, value_im)
    left_im = precise_dot(cos_table, value_im) + precise_dot(sin_table, value_re)
    right_re = precise_dot(left_re, cos_table) - precise_dot(left_im, sin_table)
    right_im = precise_dot(left_re, sin_table) + precise_dot(left_im, cos_table)
    return (right_re, right_im)


def one_position(
    window_block, probe_re, probe_im, prop_re, prop_im, measured, weight, cos_table, sin_table
):
    slices = window_block.shape[0]
    wave_re, wave_im = (probe_re, probe_im)
    waves = []
    far_re, far_im = (wave_re, wave_im)
    for s in range(slices):
        waves.append((wave_re, wave_im))
        trans_re, trans_im = (window_block[s, 0], window_block[s, 1])
        exit_re = wave_re * trans_re - wave_im * trans_im
        exit_im = wave_re * trans_im + wave_im * trans_re
        if s < slices - 1:
            spec_re, spec_im = transform(exit_re, exit_im, cos_table, sin_table)
            spec_re, spec_im = (
                spec_re * prop_re - spec_im * prop_im,
                spec_re * prop_im + spec_im * prop_re,
            )
            wave_re, wave_im = transform(spec_re, spec_im, cos_table, -sin_table)
        else:
            far_re, far_im = transform(exit_re, exit_im, cos_table, sin_table)
    residual = far_re * far_re + far_im * far_im - measured
    back_re, back_im = transform(
        2.0 * weight * residual * far_re, 2.0 * weight * residual * far_im, cos_table, -sin_table
    )
    terms = [None] * slices
    probe_term = None
    for s in reversed(range(slices)):
        wave_re, wave_im = waves[s]
        trans_re, trans_im = (window_block[s, 0], window_block[s, 1])
        terms[s] = jnp.stack(
            [wave_re * back_re + wave_im * back_im, wave_re * back_im - wave_im * back_re]
        )
        carry_re = trans_re * back_re + trans_im * back_im
        carry_im = trans_re * back_im - trans_im * back_re
        if s > 0:
            spec_re, spec_im = transform(carry_re, carry_im, cos_table, sin_table)
            spec_re, spec_im = (
                spec_re * prop_re + spec_im * prop_im,
                spec_im * prop_re - spec_re * prop_im,
            )
            back_re, back_im = transform(spec_re, spec_im, cos_table, -sin_table)
        else:
            probe_term = jnp.stack([carry_re, carry_im])
    return (jnp.stack(terms), probe_term)


def return_rows(gradient, margin):
    upper_rim = gradient[:, :, :margin, :]
    lower_rim = gradient[:, :, gradient.shape[2] - margin :, :]
    interior = gradient[:, :, margin : gradient.shape[2] - margin, :]
    from_below = passed_along(upper_rim, "sy", -1)
    from_above = passed_along(lower_rim, "sy", 1)
    interior = interior.at[:, :, interior.shape[2] - margin :, :].add(from_below)
    return interior.at[:, :, :margin, :].add(from_above)


def return_columns(gradient, margin):
    left_rim = gradient[:, :, :, :margin]
    right_rim = gradient[:, :, :, gradient.shape[3] - margin :]
    interior = gradient[:, :, :, margin : gradient.shape[3] - margin]
    from_right = passed_along(left_rim, "sx", -1)
    from_left = passed_along(right_rim, "sx", 1)
    interior = interior.at[:, :, :, interior.shape[3] - margin :].add(from_right)
    return interior.at[:, :, :, :margin].add(from_left)


def shards(object_slices, probe_wave, propagator_phase, intensities, scan_offsets, live_counts):
    window = probe_wave.shape[-1]
    margin = window // 2
    slices = object_slices.shape[0]
    slot_count = scan_offsets.shape[2]
    cos_table, sin_table = dft_tables(window)
    prop_re = jnp.cos(propagator_phase)
    prop_im = jnp.sin(propagator_phase)
    extended = with_halo(object_slices, (("sy", 2), ("sx", 3)), margin)
    offsets = scan_offsets[0, 0]
    measured_all = intensities[0, 0]
    live_total = live_counts[0, 0]
    zero = jnp.int32(0)

    def visit(position, carried, weight):
        gradient, probe_sum = carried
        row_here = offsets[position, 0]
        col_here = offsets[position, 1]
        window_block = lax.dynamic_slice(
            extended, (zero, zero, row_here, col_here), (slices, 2, window, window)
        ).astype(jnp.float32)
        measured = lax.dynamic_index_in_dim(measured_all, position, 0, keepdims=False).astype(
            jnp.float32
        )
        grad_window, grad_probe = one_position(
            window_block,
            probe_wave[0],
            probe_wave[1],
            prop_re,
            prop_im,
            measured,
            weight,
            cos_table,
            sin_table,
        )
        current = lax.dynamic_slice(
            gradient, (zero, zero, row_here, col_here), (slices, 2, window, window)
        )
        gradient = lax.dynamic_update_slice(
            gradient, current + grad_window, (zero, zero, row_here, col_here)
        )
        return (gradient, probe_sum + grad_probe)

    start = (jnp.zeros(extended.shape, jnp.float32), jnp.zeros((2, window, window), jnp.float32))

    def every_slot(position, carried):
        weight = jnp.where(position < live_total, 1.0, 0.0).astype(jnp.float32)
        return visit(position, carried, weight)

    gradient, probe_sum = lax.fori_loop(0, slot_count, every_slot, start)
    gradient = return_columns(return_rows(gradient, margin), margin)
    scale = 1.0 / math.sqrt(slot_count * lax.axis_size("sy") * lax.axis_size("sx"))
    probe_gradient = lax.psum(probe_sum, ("sy", "sx")) * scale
    return (gradient, probe_gradient)


def solution(mesh):
    return jax.shard_map(
        shards,
        mesh=mesh,
        in_specs=(
            P(None, None, "sy", "sx"),
            P(),
            P(),
            P("sy", "sx", None, None, None),
            P("sy", "sx", None, None),
            P("sy", "sx"),
        ),
        out_specs=(P(None, None, "sy", "sx"), P()),
        check_vma=False,
    )
```

profile of v0, /device:TPU:0, one launch (start us, length us, event | category | flops | bytes accessed | tf_op | source)
XLA Modules:
  0.0 643.9 jit_solution(3217993733628233518)
XLA Ops:
  7.2 4.9 collective-permute-start
  13.4 43.8 %collective-permute-done = bf16[2,2,128,1024]{3,2,1,0:T(8,128)(2,1)S(1)} collective-permute-done((bf16[2,2,128,1024]{3,2,1,0:T(8,128)(2,1)}, bf16[2,2,128,1024]{3,2,1,0:T(8,128)(2,1)S(1)}, u32[]{:S(2)}, u32[]{:S(2)}) %collective-permute-start) | collective-permute-done | bytes 1048608 | tf_op jit(solution)/shard_map/ppermute | solution.py:23
  58.3 2.3 constant_dynamic-update-slice_fusion.1
  67.8 3.5 pad_maximum_fusion
  71.3 3.7 broadcast_in_dim.8
  75.1 379.3 %while.24 = (s32[]{:T(128)}, f32[2,2,384,1280]{3,2,1,0:T(8,128)}, f32[2,256,256]{2,1,0:T(8,128)S(1)}, s32[4,2]{0,1:T(2,128)S(1)}, f32[2,256,256]{2,1,0:T(8,128)S...) while((s32[]{:T(128)}, f32[2,2,384,1280]{3,2,1,0:T(8,128)}, ...), condition=%wide.region_1.2_spmd.clone.clone, body=%wide.region_0.1_spmd.clone.clone.sunk | while | flops 9719644160 | bytes 52691288 | solution.py:168
  86.6 1.5 convolution_add_fusion.22
  92.5 2.0 multiply_add_fusion.6
  99.0 1.5 convolution_add_fusion.23
  105.0 1.7 multiply_add_fusion.7
  117.0 1.7 convolution_subtract_fusion.26
  118.7 1.5 fusion.516
  120.3 1.5 convolution_add_fusion.26
  121.8 1.5 fusion.514
  123.3 1.5 convolution_subtract_fusion.27
  129.3 2.0 multiply_subtract_fusion.6
  141.6 1.7 multiply_subtract_fusion.7
  153.6 1.8 add_bitcast_fusion.3
  155.5 1.8 maximum_add_fusion.4
  157.5 12.0 %dynamic_update_slice.11 = f32[2,2,384,1280]{3,2,1,0:T(8,128)} dynamic-update-slice(f32[2,2,384,1280]{3,2,1,0:T(8,128)} %get-tuple-element.747, f32[2,2,256,256]{3,2,1,0:T(8,128)S(1)} %maximum_add_fusion.4, s32[]{:T(128)} %constant.203.clone.1..sunk, s32[]{:T(128)} %constant.203.clone.1..sunk, s32[]{:T(128)S(6)} %select_n.326, s32[]{:T(128)S(6)} %select_n.327) | dynamic-update-slice | bytes 2097156 | tf_op jit(solution)/shard_map/while/body/eval_jaxpr/dynamic_update_slice | solution.py:157
  187.2 1.7 multiply_add_fusion.6
  199.2 1.7 multiply_add_fusion.7
  211.3 1.9 convolution_subtract_fusion.26
  213.2 1.5 fusion.516
  214.8 1.5 convolution_add_fusion.26
  216.3 1.5 fusion.514
  217.8 1.5 convolution_subtract_fusion.27
  223.8 1.7 multiply_subtract_fusion.6
  235.9 1.7 multiply_subtract_fusion.7
  248.0 2.0 add_bitcast_fusion.3
  250.0 1.8 maximum_add_fusion.4
  252.0 12.0 %dynamic_update_slice.11 = f32[2,2,384,1280]{3,2,1,0:T(8,128)} dynamic-update-slice(f32[2,2,384,1280]{3,2,1,0:T(8,128)} %get-tuple-element.747, f32[2,2,256,256]{3,2,1,0:T(8,128)S(1)} %maximum_add_fusion.4, s32[]{:T(128)} %constant.203.clone.1..sunk, s32[]{:T(128)} %constant.203.clone.1..sunk, s32[]{:T(128)S(6)} %select_n.326, s32[]{:T(128)S(6)} %select_n.327) | dynamic-update-slice | bytes 2097156 | tf_op jit(solution)/shard_map/while/body/eval_jaxpr/dynamic_update_slice | solution.py:157
  281.4 1.7 multiply_add_fusion.6
  293.5 1.9 multiply_add_fusion.7
  305.8 1.7 convolution_subtract_fusion.26
  307.4 1.5 fusion.516
  309.0 1.5 convolution_add_fusion.26
  310.5 1.5 fusion.514
  312.0 1.5 convolution_subtract_fusion.27
  318.0 1.8 multiply_subtract_fusion.6
  330.1 1.9 multiply_subtract_fusion.7
  342.4 1.7 add_bitcast_fusion.3
  344.2 1.8 maximum_add_fusion.4
  346.2 11.7 %dynamic_update_slice.11 = f32[2,2,384,1280]{3,2,1,0:T(8,128)} dynamic-update-slice(f32[2,2,384,1280]{3,2,1,0:T(8,128)} %get-tuple-element.747, f32[2,2,256,256]{3,2,1,0:T(8,128)S(1)} %maximum_add_fusion.4, s32[]{:T(128)} %constant.203.clone.1..sunk, s32[]{:T(128)} %constant.203.clone.1..sunk, s32[]{:T(128)S(6)} %select_n.326, s32[]{:T(128)S(6)} %select_n.327) | dynamic-update-slice | bytes 2097156 | tf_op jit(solution)/shard_map/while/body/eval_jaxpr/dynamic_update_slice | solution.py:157
  375.4 1.9 multiply_add_fusion.6
  387.7 1.7 multiply_add_fusion.7
  399.8 1.7 convolution_subtract_fusion.26
  401.5 1.5 fusion.516
  403.0 1.5 convolution_add_fusion.26
  404.5 1.5 fusion.514
  406.1 1.5 convolution_subtract_fusion.27
  412.0 2.0 multiply_subtract_fusion.6
  424.4 1.7 multiply_subtract_fusion.7
  436.4 1.8 add_bitcast_fusion.3
  438.3 1.8 maximum_add_fusion.4
  440.2 12.0 %dynamic_update_slice.11 = f32[2,2,384,1280]{3,2,1,0:T(8,128)} dynamic-update-slice(f32[2,2,384,1280]{3,2,1,0:T(8,128)} %get-tuple-element.747, f32[2,2,256,256]{3,2,1,0:T(8,128)S(1)} %maximum_add_fusion.4, s32[]{:T(128)} %constant.203.clone.1..sunk, s32[]{:T(128)} %constant.203.clone.1..sunk, s32[]{:T(128)S(6)} %select_n.326, s32[]{:T(128)S(6)} %select_n.327) | dynamic-update-slice | bytes 2097156 | tf_op jit(solution)/shard_map/while/body/eval_jaxpr/dynamic_update_slice | solution.py:157
  454.3 5.4 fusion.304
  461.0 6.1 collective-permute-start.5
  467.2 55.8 %collective-permute-done.4 = f32[2,2,128,1280]{3,2,1,0:T(8,128)} collective-permute-done((f32[2,2,128,1280]{3,2,1,0:T(8,128)}, f32[2,2,128,1280]{3,2,1,0:T(8,128)}, u32[]{:S(2)}, u32[]{:S(2)}) %collective-permute-start.4) | collective-permute-done | bytes 2621472 | tf_op jit(solution)/shard_map/ppermute | solution.py:12
  523.0 53.3 %collective-permute-done.5 = f32[2,2,128,1280]{3,2,1,0:T(8,128)} collective-permute-done((f32[2,2,128,1280]{3,2,1,0:T(8,128)}, f32[2,2,128,1280]{3,2,1,0:T(8,128)}, u32[]{:S(2)}, u32[]{:S(2)}) %collective-permute-start.5) | collective-permute-done | bytes 2621472 | tf_op jit(solution)/shard_map/ppermute | solution.py:12
  576.3 3.8 add_add_fusion
  582.1 3.1 collective-permute-start.7
  585.2 47.9 %all-reduce.2.cloned.1.call-done = f32[2,256,256]{2,1,0:T(8,128)} async-done(((f32[2,256,256]{2,1,0:T(8,128)}), f32[2,256,256]{2,1,0:T(8,128)}) %all-reduce.2.cloned.1.call-update) | async-done | bytes 524304 | tf_op jit(solution)/shard_map/psum | solution.py:171
  633.1 1.9 broadcast_multiply_fusion
  (203 shorter events, 245.2 us)
Async XLA Ops:
  7.2 625.9 %all-reduce.2.cloned.1.call-start = ((), (), s32[]{:S(2)}) async-start(), calls=%async_computation | async-start | bytes 1048576 | tf_op jit(solution)/shard_map/psum | solution.py:171
  7.2 50.0 %collective-permute-start = (bf16[2,2,128,1024]{3,2,1,0:T(8,128)(2,1)}, bf16[2,2,128,1024]{3,2,1,0:T(8,128)(2,1)S(1)}, u32[]{:S(2)}, u32[]{:S(2)}) collective-permute-start(bf16[2,2,128,1024]{3,2,1,0:T(8,128)(2,1)} %param.20), channel_id=1, source_target_pairs={{0,2},{2,4},{4,6},{6,8},{8,10},{10,12},{12,14},{14,16},{16,18},{18... | collective-permute-start | bytes 3145736 | tf_op jit(solution)/shard_map/ppermute | solution.py:23
  12.1 48.5 %collective-permute-start.1 = (bf16[2,2,128,1024]{3,2,1,0:T(8,128)(2,1)}, bf16[2,2,128,1024]{3,2,1,0:T(8,128)(2,1)S(1)}, u32[]{:S(2)}, u32[]{:S(2)}) collective-permute-start(bf16[2,2,128,1024]{3,2,1,0:T(8,128)(2,1)} %param.20), channel_id=1, source_target_pairs={{2,0},{4,2},{6,4},{8,6},{10,8},{12,10},{14,12},{16,14},{18,16},{20... | collective-permute-start | bytes 3145736 | tf_op jit(solution)/shard_map/ppermute | solution.py:25
  58.3 7.2 %copy-start.3 = (f32[256,256]{1,0:T(8,128)S(1)}, f32[256,256]{1,0:T(8,128)}, u32[]{:S(2)}) copy-start(f32[256,256]{1,0:T(8,128)} %param.22) | copy-start | bytes 786436
  62.9 3.6 collective-permute-start.2
  64.2 3.6 collective-permute-start.3
  71.3 3.7 copy-start
  71.3 3.7 copy-start.4
  71.3 3.7 copy-start.5
  454.3 5.4 copy-start.1
  459.7 63.3 %collective-permute-start.4 = (f32[2,2,128,1280]{3,2,1,0:T(8,128)}, f32[2,2,128,1280]{3,2,1,0:T(8,128)}, u32[]{:S(2)}, u32[]{:S(2)}) collective-permute-start(f32[2,2,128,1280]{3,2,1,0:T(8,128)} %get-tuple-element.618), channel_id=1, source_target_pairs={{2,0},{4,2},{6,4},{8,6},{10,8},{12,10},{14,12},{16,14},{18,16},{20... | collective-permute-start | bytes 7864328 | tf_op jit(solution)/shard_map/ppermute | solution.py:12
  461.0 115.3 %collective-permute-start.5 = (f32[2,2,128,1280]{3,2,1,0:T(8,128)}, f32[2,2,128,1280]{3,2,1,0:T(8,128)}, u32[]{:S(2)}, u32[]{:S(2)}) collective-permute-start(f32[2,2,128,1280]{3,2,1,0:T(8,128)} %get-tuple-element.619), channel_id=1, source_target_pairs={{0,2},{2,4},{4,6},{6,8},{8,10},{10,12},{12,14},{14,16},{16,18},{18... | collective-permute-start | bytes 7864328 | tf_op jit(solution)/shard_map/ppermute | solution.py:12
  580.9 54.4 %collective-permute-start.6 = (f32[2,2,128,128]{3,2,1,0:T(8,128)}, f32[2,2,128,128]{3,2,1,0:T(8,128)S(1)}, u32[]{:S(2)}, u32[]{:S(2)}) collective-permute-start(f32[2,2,128,128]{3,2,1,0:T(8,128)} %get-tuple-element.623), channel_id=1, source_target_pairs={{1,0},{3,2},{5,4},{7,6},{9,8},{11,10},{13,12},{15,14},{17,16},{19,... | collective-permute-start | bytes 786440 | tf_op jit(solution)/shard_map/ppermute | solution.py:12
  582.1 53.2 %collective-permute-start.7 = (f32[2,2,128,128]{3,2,1,0:T(8,128)S(1)}, f32[2,2,128,128]{3,2,1,0:T(8,128)S(1)}, u32[]{:S(2)}, u32[]{:S(2)}) collective-permute-start(f32[2,2,128,128]{3,2,1,0:T(8,128)S(1)} %get-tuple-element.622), channel_id=1, source_target_pairs={{0,1},{2,3},{4,5},{6,7},{8,9},{10,11},{12,13},{14,15},{16,17},{18,... | collective-permute-start | bytes 786440 | tf_op jit(solution)/shard_map/ppermute | solution.py:12
  635.4 1.3 copy-start.2
Sparse Core Ops, SparseCore 0:
  467.3 165.6 all-reduce.1
where the time goes:
time: 649 us; the launch traced here: 644 us
  matrix products  291 us (45%)
  waiting for transfers between devices  202 us (31%)
  local copies, waits for them, and re-layouts  68.4 us (11%)
  other arithmetic  23.6 us (4%)
  loops' own time  23.3 us (4%)
  starting transfers between devices  20.6 us (3%)
  between operations  14.5 us (2%)
    dot_general x192, matrix products, precise_dot(): jnp.dot(left, right, precision=lax.Precision.HIGHEST, preferred_element_t...  291 us
    ppermute x4, waiting for transfers between devices, passed_along(): return lax.ppermute(block, axis, route)  109 us
    psum x1, waiting for transfers between devices, shards(): probe_gradient = lax.psum(probe_sum, ('sy', 'sx')) * scale  47.9 us
    dynamic_update_slice x4, local copies, waits for them, and re-layouts, visit(): lax.dynamic_update_slice(gradient, current + grad_window, (zero, zero, ro...  47.7 us
    ppermute x2, waiting for transfers between devices, with_halo(): lax.ppermute(tail, axis, [(i, (i + 1) % count) for i in range(ends)])  43.8 us
    another operation x1, loops' own time, shards(): gradient, probe_sum = lax.fori_loop(0, slot_count, every_slot, start)  23.3 us
  transfers between devices with their start and end apart: 9, of which 5 were waited for; matrix products, arithmetic and copies ran while one was open for 2% of the time, Pallas kernels for 0%

commit v1 on v0

v1 whole, which is shorter than its diff:
```python
import functools
import math

import jax
import jax.numpy as jnp
import numpy as np
from jax import lax
from jax.experimental import pallas as pl
from jax.experimental.pallas import tpu as pltpu
from jax.sharding import PartitionSpec as P

F32 = jnp.float32
BF16 = jnp.bfloat16
WHOLE = pl.BlockSpec(memory_space=pltpu.VMEM)
SCALARS = pl.BlockSpec(memory_space=pltpu.SMEM)


def passed_along(block, axis, distance):
    devices = range(lax.axis_size(axis))
    route = [(i - distance, i) for i in devices if i - distance in devices]
    return lax.ppermute(block, axis, route)


def split_tables(window):
    half = window // 2
    steps = np.arange(half)
    left, right = [], []

    def parts(matrix):
        high = matrix.astype(np.float32).astype(jnp.bfloat16)
        low = (matrix - high.astype(np.float64)).astype(np.float32).astype(jnp.bfloat16)
        return high, low

    forms = []
    for odd in (0, 1):
        angle = -2.0 * math.pi / window * ((steps[None, :] * (2 * steps[:, None] + odd)) % window)
        re, im = np.cos(angle) / math.sqrt(window), np.sin(angle) / math.sqrt(window)
        forms.append(np.block([[re, -im], [im, re]]))
    for turn in (0, 1):
        for form in forms:
            high, low = parts(form.T if turn else form)
            left.append(np.concatenate([high, high, low], 1))
            high, low = parts(form if turn else form.T)
            right.append(np.concatenate([high, high, low], 0))
    return np.stack(left), np.stack(right)


def halves(value):
    high = value.astype(BF16)
    low = (value - high.astype(F32)).astype(BF16)
    return high, low


def left_dot(table, value):
    high, low = halves(value)
    return jnp.dot(table, jnp.concatenate([high, low, high], 0), preferred_element_type=F32)


def right_dot(value, table):
    high, low = halves(value)
    return jnp.dot(jnp.concatenate([high, low, high], 1), table, preferred_element_type=F32)


def rows_cat(a, b):
    return jnp.concatenate([a, b], 0)


def lanes_cat(a, b):
    return jnp.concatenate([a, b], 1)


def forward(re, im, left, right):
    h = re.shape[0] // 2
    even = left_dot(left[0], rows_cat(re[:h] + re[h:], im[:h] + im[h:]))
    odd = left_dot(left[1], rows_cat(re[:h] - re[h:], im[:h] - im[h:]))
    re, im = rows_cat(even[:h], odd[:h]), rows_cat(even[h:], odd[h:])
    even = right_dot(lanes_cat(re[:, :h] + re[:, h:], im[:, :h] + im[:, h:]), right[0])
    odd = right_dot(lanes_cat(re[:, :h] - re[:, h:], im[:, :h] - im[:, h:]), right[1])
    return lanes_cat(even[:, :h], odd[:, :h]), lanes_cat(even[:, h:], odd[:, h:])


def backward(re, im, left, right):
    h = re.shape[0] // 2
    even = left_dot(left[2], rows_cat(re[:h], im[:h]))
    odd = left_dot(left[3], rows_cat(re[h:], im[h:]))
    plus, minus = even + odd, even - odd
    re, im = rows_cat(plus[:h], minus[:h]), rows_cat(plus[h:], minus[h:])
    even = right_dot(lanes_cat(re[:, :h], im[:, :h]), right[2])
    odd = right_dot(lanes_cat(re[:, h:], im[:, h:]), right[3])
    plus, minus = even + odd, even - odd
    return lanes_cat(plus[:, :h], minus[:, :h]), lanes_cat(plus[:, h:], minus[:, h:])


def place(offsets, q):
    row, col = offsets[q, 0], offsets[q, 1]
    start = pl.multiple_of((col // 128) * 128, 128)
    return row, start, col - start


def read_window(field, offsets, q, window):
    row, start, lane = place(offsets, q)
    rows, span = field.shape[1], window + 128
    found = []
    for p in range(2):
        block = field[p, :, pl.ds(start, span)].astype(F32)
        block = pltpu.roll(block, lax.rem(span - lane, span), 1)[:, :window]
        found.append(pltpu.roll(block, lax.rem(rows - row, rows), 0)[:window])
    return found


def add_window(field, offsets, q, terms):
    row, start, lane = place(offsets, q)
    window = terms[0].shape[0]
    rows, span = field.shape[1], window + 128
    for p in range(2):
        block = jnp.concatenate([terms[p], jnp.zeros((rows - window, window), F32)], 0)
        block = pltpu.roll(block, row, 0)
        block = jnp.concatenate([block, jnp.zeros((rows, span - window), F32)], 1)
        field[p, :, pl.ds(start, span)] += pltpu.roll(block, lane, 1)


def first_kernel(offsets, live, field, probe, prop, left, right, wave, trans):
    window = probe.shape[-1]

    def slot(q, _):
        t_re, t_im = read_window(field, offsets, q, window)
        trans[q, 0] = t_re.astype(BF16)
        trans[q, 1] = t_im.astype(BF16)
        p_re, p_im = probe[0], probe[1]
        re, im = forward(p_re * t_re - p_im * t_im, p_re * t_im + p_im * t_re, left, right)
        h_re, h_im = prop[0], prop[1]
        re, im = backward(re * h_re - im * h_im, re * h_im + im * h_re, left, right)
        wave[q, 0] = re
        wave[q, 1] = im
        return 0

    lax.fori_loop(0, live[0, 0], slot, 0)


def middle_kernel(offsets, live, field, wave, measured, left, right, gradient, carry):
    window = wave.shape[-1]
    gradient[...] = jnp.zeros(gradient.shape, F32)

    def slot(q, _):
        t_re, t_im = read_window(field, offsets, q, window)
        w_re, w_im = wave[q, 0], wave[q, 1]
        re, im = forward(w_re * t_re - w_im * t_im, w_re * t_im + w_im * t_re, left, right)
        residual = 2.0 * (re * re + im * im - measured[q].astype(F32))
        re, im = backward(residual * re, residual * im, left, right)
        w_re, w_im = wave[q, 0], wave[q, 1]
        add_window(gradient, offsets, q, (w_re * re + w_im * im, w_re * im - w_im * re))
        carry[q, 0] = t_re * re + t_im * im
        carry[q, 1] = t_re * im - t_im * re
        return 0

    lax.fori_loop(0, live[0, 0], slot, 0)


def last_kernel(offsets, live, carry, trans, probe, prop, left, right, gradient, total):
    gradient[...] = jnp.zeros(gradient.shape, F32)
    total[...] = jnp.zeros(total.shape, F32)

    def slot(q, _):
        re, im = forward(carry[q, 0], carry[q, 1], left, right)
        h_re, h_im = prop[0], prop[1]
        re, im = backward(re * h_re + im * h_im, im * h_re - re * h_im, left, right)
        p_re, p_im = probe[0], probe[1]
        add_window(gradient, offsets, q, (p_re * re + p_im * im, p_re * im - p_im * re))
        t_re, t_im = trans[q, 0].astype(F32), trans[q, 1].astype(F32)
        total[0] += t_re * re + t_im * im
        total[1] += t_re * im - t_im * re
        return 0

    lax.fori_loop(0, live[0, 0], slot, 0)


def call(kernel, outs, name, flops, *args):
    moved = sum(math.prod(a.shape) * a.dtype.itemsize for a in (*args, *outs))
    return pl.pallas_call(
        kernel,
        out_shape=outs,
        in_specs=[SCALARS] * 2 + [WHOLE] * (len(args) - 2),
        out_specs=[WHOLE] * len(outs),
        compiler_params=pltpu.CompilerParams(vmem_limit_bytes=48 * 1024 * 1024),
        cost_estimate=pl.CostEstimate(flops=flops, bytes_accessed=moved, transcendentals=0),
        name=name,
    )(*args)


def halo_rows(cells):
    above = passed_along(cells, "sy", 1)
    below = passed_along(cells, "sy", -1)
    return jnp.concatenate([above, cells, below], 1)


def halo_columns(cells, margin):
    from_left = passed_along(cells[:, :, cells.shape[2] - margin :], "sx", 1)
    from_right = passed_along(cells[:, :, :margin], "sx", -1)
    return jnp.concatenate([from_left, cells, from_right], 2)


def coded(block):
    top = jnp.max(jnp.abs(block), axis=1, keepdims=True)
    step = top * (1.0 / 32767.0)
    inverse = jnp.where(top > 1e-30, 32767.0 / jnp.where(top > 1e-30, top, 1.0), 0.0)
    return jnp.round(block * inverse).astype(jnp.int16), step


def sent_rows(block, distance):
    code, step = coded(block)
    code, step = passed_along(code, "sy", distance), passed_along(step, "sy", distance)
    return code.astype(F32) * step


def returned(gradient, margin):
    wide = gradient.shape[2]
    to_left, to_right = gradient[:, :, :margin], gradient[:, :, wide - margin :]
    from_right = passed_along(to_left, "sx", -1)
    from_left = passed_along(to_right, "sx", 1)
    inner = gradient[:, :, margin : wide - margin]
    inner = jnp.concatenate(
        [
            inner[:, :, :margin] + from_left,
            inner[:, :, margin:-margin],
            inner[:, :, -margin:] + from_right,
        ],
        2,
    )
    above, own, below = inner[:, :margin], inner[:, margin : 2 * margin], inner[:, 2 * margin :]
    return own + sent_rows(above, -1) + sent_rows(below, 1)


def shards(object_slices, probe_wave, propagator_phase, intensities, scan_offsets, live_counts):
    window = probe_wave.shape[-1]
    half = window // 2
    slots = scan_offsets.shape[2]
    offsets = scan_offsets[0, 0]

    first_field = halo_rows(object_slices[0])
    second_cells, first_field = lax.optimization_barrier((object_slices[1], first_field))
    second_field = halo_rows(second_cells)
    first_field = halo_columns(first_field, half)
    second_field = halo_columns(second_field, half)

    left, right = split_tables(window)
    left, right = jnp.asarray(left), jnp.asarray(right)
    order = np.concatenate([np.arange(0, window, 2), np.arange(1, window, 2)])
    pick = jnp.asarray(np.eye(window)[order], BF16)
    measured = jnp.einsum(
        "aj,qjk->qak", pick, intensities[0, 0], preferred_element_type=F32
    ).astype(BF16)
    measured = jnp.einsum("qak,bk->qab", measured, pick, preferred_element_type=F32).astype(BF16)
    phase = propagator_phase.reshape(half, 2, half, 2).transpose(1, 0, 3, 2).reshape(window, window)
    prop = jnp.stack([jnp.cos(phase), jnp.sin(phase)])

    flops = slots * 24 * 2 * window**3
    per_slot = jax.ShapeDtypeStruct((slots, 2, window, window), F32)
    per_slot_short = jax.ShapeDtypeStruct((slots, 2, window, window), BF16)
    whole_field = jax.ShapeDtypeStruct(first_field.shape, F32)
    pair = jax.ShapeDtypeStruct((2, window, window), F32)
    wave, trans = call(
        first_kernel, [per_slot, per_slot_short], "first", flops,
        offsets, live_counts, first_field, probe_wave, prop, left, right,
    )
    second_gradient, carry = call(
        middle_kernel, [whole_field, per_slot], "middle", flops,
        offsets, live_counts, second_field, wave, measured, left, right,
    )
    first_gradient, total = call(
        last_kernel, [whole_field, pair], "last", flops,
        offsets, live_counts, carry, trans, probe_wave, prop, left, right,
    )
    scale = 1.0 / math.sqrt(slots * lax.axis_size("sy") * lax.axis_size("sx"))
    probe_gradient = lax.psum(total, ("sy", "sx")) * scale
    gradient = jnp.stack([returned(first_gradient, half), returned(second_gradient, half)])
    return (gradient, probe_gradient)


def solution(mesh):
    return jax.shard_map(
        shards,
        mesh=mesh,
        in_specs=(
            P(None, None, "sy", "sx"),
            P(),
            P(),
            P("sy", "sx", None, None, None),
            P("sy", "sx", None, None),
            P("sy", "sx"),
        ),
        out_specs=(P(None, None, "sy", "sx"), P()),
        check_vma=False,
    )
```

time: 649 us -> 315 us (0.49)
  matrix products: 291 us -> 0.5 us
  waiting for transfers between devices: 202 us -> 127 us
  starting transfers between devices: 20.6 us -> 64.1 us
  loops' own time: 23.3 us -> 0 us
  Pallas kernels: 0 us -> 18.1 us
    dot_general x192 -> x1, matrix products: 291 us -> 0.5 us  [shards(): jnp.einsum('qak,bk->qab', measured, pick, preferred_element_type=F32)]
    ppermute x4 -> x20, waiting for transfers between devices: 109 us -> 17.6 us  [passed_along(): return lax.ppermute(block, axis, route)]
    psum x1, waiting for transfers between devices: 47.9 us -> 109 us  [shards(): probe_gradient = lax.psum(total, ('sy', 'sx')) * scale]
    ppermute x4 -> x20, starting transfers between devices: 11.8 us -> 64 us  [passed_along(): return lax.ppermute(block, axis, route)]
    dynamic_update_slice x4 -> x0, local copies, waits for them, and re-layouts: 47.7 us -> none  [visit(): lax.dynamic_update_slice(gradient, current + grad_window, (zero, zero, ro...]
    ppermute x4 -> x0, waiting for transfers between devices: 45.1 us -> none  [the longest x2 43.8 us: with_halo(): lax.ppermute(tail, axis, [(i, (i + 1) % count) for i in range(ends)])]
    sin x1 -> x4, local copies, waits for them, and re-layouts: 0.97 us -> 29.6 us  [shards(): prop = jnp.stack([jnp.cos(phase), jnp.sin(phase)])]
    cos x0 -> x3, local copies, waits for them, and re-layouts: none -> 27.8 us  [shards(): prop = jnp.stack([jnp.cos(phase), jnp.sin(phase)])]
  transfers between devices with their start and end apart: 9 -> 21, of which waited for: 5 -> 4; matrix products, arithmetic and copies ran while one was open for 2% -> 25% of each run, Pallas kernels for 0% -> 2%
where the time goes in v1:
time: 315 us; the launch traced here: 314 us
  waiting for transfers between devices  127 us (40%)
  local copies, waits for them, and re-layouts  69.4 us (22%)
  starting transfers between devices  64.1 us (20%)
  other arithmetic  19.7 us (6%)
  Pallas kernels  18.1 us (6%)
  between operations  15.2 us (5%)
    psum x1, waiting for transfers between devices, shards(): probe_gradient = lax.psum(total, ('sy', 'sx')) * scale  109 us
    ppermute x20, starting transfers between devices, passed_along(): return lax.ppermute(block, axis, route)  64 us
    sin x4, local copies, waits for them, and re-layouts, shards(): prop = jnp.stack([jnp.cos(phase), jnp.sin(phase)])  29.6 us
    cos x3, local copies, waits for them, and re-layouts, shards(): prop = jnp.stack([jnp.cos(phase), jnp.sin(phase)])  27.8 us
    pallas_call x3, Pallas kernels, call(): pl.pallas_call(kernel, out_shape=outs, in_specs=[SCALARS] * 2 + [WHOLE] *...  18.1 us
    ppermute x20, waiting for transfers between devices, passed_along(): return lax.ppermute(block, axis, route)  17.6 us
  transfers between devices with their start and end apart: 21, of which 4 were waited for; matrix products, arithmetic and copies ran while one was open for 25% of the time, Pallas kernels for 2%

profile of v1, /device:TPU:0, one launch (start us, length us, event | category | flops | bytes accessed | tf_op | source)
XLA Modules:
  0.0 313.9 jit_solution(2872972079855858063)
XLA Ops:
  7.2 0.0 all-reduce.2.cloned.1.call-start
  7.2 2.1 slice_bitcast_fusion
  9.3 4.9 %collective-permute-start = (bf16[2,128,1024]{2,1,0:T(8,128)(2,1)S(1)}, bf16[2,128,1024]{2,1,0:T(8,128)(2,1)S(1)}, u32[]{:S(2)}, u32[]{:S(2)}) collective-permute-start(bf16[2,128,1024]{2,1,0:T(8,128)(2,1)S(1)} %get-tuple-element.34), channel_id=1, source_target_pairs={{0,2},{2,4},{4,6},{6,8},{8,10},{10,12},{12,14},{14,16},{16,18},{18... | collective-permute-start | bytes 1572872 | tf_op jit(solution)/shard_map/ppermute | solution.py:21
  14.2 1.3 collective-permute-start.1
  15.5 1.9 fusion.9
  17.4 18.1 %cos.20 = f32[128,2,128,2]{3,2,1,0:T(8,128)} reshape(f32[256,256]{1,0:T(8,128)S(1)} %get-tuple-element.37) | data formatting | bytes 524288 | tf_op jit(solution)/shard_map/cos | solution.py:254
  35.4 9.5 %copy.16 = f32[2,128,2,128]{3,2,1,0:T(2,128)S(1)} copy(f32[2,128,2,128]{2,3,0,1:T(8,128)} %bitcast.34) | data formatting | bytes 524288 | tf_op jit(solution)/shard_map/cos | solution.py:254
  44.9 0.2 cos.22
  45.2 18.1 %sin.20 = f32[128,2,128,2]{3,2,1,0:T(8,128)} reshape(f32[256,256]{1,0:T(8,128)S(1)} %get-tuple-element.36) | data formatting | bytes 524288 | tf_op jit(solution)/shard_map/sin | solution.py:254
  63.2 9.5 %copy.17 = f32[2,128,2,128]{3,2,1,0:T(2,128)S(1)} copy(f32[2,128,2,128]{2,3,0,1:T(8,128)} %bitcast.35) | data formatting | bytes 524288 | tf_op jit(solution)/shard_map/sin | solution.py:254
  72.8 0.2 sin.22
  73.0 0.1 copy.20.offsets
  73.8 0.8 copy-done.10
  74.6 1.4 pad_maximum_fusion.5
  76.0 5.4 %collective-permute-start.2 = (bf16[2,128,1024]{2,1,0:T(8,128)(2,1)}, bf16[2,128,1024]{2,1,0:T(8,128)(2,1)}, u32[]{:S(2)}, u32[]{:S(2)}) collective-permute-start(bf16[2,128,1024]{2,1,0:T(8,128)(2,1)} %get-tuple-element.10), channel_id=1, source_target_pairs={{0,2},{2,4},{4,6},{6,8},{8,10},{10,12},{12,14},{14,16},{16,18},{18... | collective-permute-start | bytes 1572872 | tf_op jit(solution)/shard_map/ppermute | solution.py:21
  81.3 0.7 fusion.7
  82.1 2.0 collective-permute-start.6
  84.0 1.3 collective-permute-start.7
  85.3 0.5 convolution_convert_fusion.measured
  85.9 1.6 collective-permute-start.3
  87.5 2.5 pad_maximum_fusion.4.field
  90.0 1.4 collective-permute-done.2
  91.4 1.1 constant_dynamic-update-slice_fusion.2
  92.5 1.1 constant_dynamic-update-slice_fusion.1
  93.6 11.8 %collective-permute-done.3 = bf16[2,128,1024]{2,1,0:T(8,128)(2,1)S(1)} collective-permute-done((bf16[2,128,1024]{2,1,0:T(8,128)(2,1)}, bf16[2,128,1024]{2,1,0:T(8,128)(2,1)S(1)}, u32[]{:S(2)}, u32[]{:S(2)}) %collective-permute-start.3) | collective-permute-done | bytes 524320 | tf_op jit(solution)/shard_map/ppermute | solution.py:21
  105.4 0.1 fusion.8
  105.5 1.3 collective-permute-start.4
  106.8 1.3 collective-permute-start.5
  108.1 4.9 %first.1 = (f32[4,2,256,256]{3,2,1,0:T(8,128)}, bf16[4,2,256,256]{3,2,1,0:T(8,128)(2,1)S(1)}) custom-call(s32[4,2]{1,0:T(4,128)S(1)} %copy.20.offsets, s32[1,1]{1,0:T(1,128)S(6)} %copy.25.live, bf16[2,384,1280]{2,1,0:T(8,128)(2,1)} %pad_maximum_fusion.4.field, f32[2,256,256]{2,1,0:T(8,128)S(1)} %copy-done.2, ...), custom_call_target="tpu_custom_call" | custom-call | flops 3221225472 | bytes 9306148 | tf_op jit(solution)/shard_map/first/pallas_call | solution.py:179
  113.0 0.2 pad_maximum_fusion.3.field
  113.2 7.0 %middle.1 = (f32[2,384,1280]{2,1,0:T(8,128)}, f32[4,2,256,256]{3,2,1,0:T(8,128)}) custom-call(s32[4,2]{1,0:T(4,128)S(1)} %copy.20.offsets, s32[1,1]{1,0:T(1,128)S(6)} %copy.25.live, bf16[2,384,1280]{2,1,0:T(8,128)(2,1)S(1)} %pad_maximum_fusion.3.field, f32[4,2,256,256]{3,2,1,0:T(8,128)} %get-tuple-element.12.wave, ...), custom_call_target="tpu_custom_call" | custom-call | flops 3221225472 | bytes 13762596 | tf_op jit(solution)/shard_map/middle/pallas_call | solution.py:179
  120.2 6.2 %last.1 = (f32[2,384,1280]{2,1,0:T(8,128)}, f32[2,256,256]{2,1,0:T(8,128)}) custom-call(s32[4,2]{1,0:T(4,128)S(1)} %copy.20.offsets, s32[1,1]{1,0:T(1,128)S(6)} %copy.25.live, f32[4,2,256,256]{3,2,1,0:T(8,128)} %get-tuple-element.13.carry, bf16[4,2,256,256]{3,2,1,0:T(8,128)(2,1)S(1)} %get-tuple-element.14.trans, f32[2,256,256]{2,1,0:T(8,128)S(1)} %copy-done.2, ...), custom_call_target="tpu_custom_call" | custom-call | flops 3221225472 | bytes 11796516 | tf_op jit(solution)/shard_map/last/pallas_call | solution.py:179
  126.4 1.0 slice.81
  127.4 9.4 %collective-permute-start.8 = (f32[2,384,128]{2,1,0:T(8,128)S(1)}, f32[2,384,128]{2,1,0:T(8,128)S(1)}, u32[]{:S(2)}, u32[]{:S(2)}) collective-permute-start(f32[2,384,128]{2,1,0:T(8,128)S(1)} %slice.81), channel_id=1, source_target_pairs={{0,1},{2,3},{4,5},{6,7},{8,9},{10,11},{12,13},{14,15},{16,17},{18,... | collective-permute-start | bytes 1179656 | tf_op jit(solution)/shard_map/ppermute | solution.py:21
  136.9 2.0 collective-permute-start.14
  138.9 1.9 slice_add_fusion.5
  140.9 1.3 collective-permute-start.9
  142.1 3.3 %slice.82 = f32[2,384,768]{2,1,0:T(8,128)} slice(f32[2,384,1280]{2,1,0:T(8,128)} %get-tuple-element.15), slice={[0:2], [0:384], [256:1024]} | slice | bytes 4718592 | tf_op jit(solution)/shard_map/slice | solution.py:224
  145.4 0.2 slice.90
  145.6 1.5 slice_add_fusion.3
  147.1 1.3 collective-permute-start.15
  148.4 1.2 slice_add_fusion.4
  149.6 0.3 pad_maximum_fusion
  149.9 0.2 abs_reduce_fusion.3
  150.2 1.6 round-nearest-even_convert_fusion.3
  151.7 1.3 collective-permute-start.10
  153.0 5.4 %collective-permute-start.12 = (s16[2,128,1024]{2,1,0:T(8,128)(2,1)S(1)}, s16[2,128,1024]{2,1,0:T(8,128)(2,1)}, u32[]{:S(2)}, u32[]{:S(2)}) collective-permute-start(s16[2,128,1024]{2,1,0:T(8,128)(2,1)S(1)} %get-tuple-element.27), channel_id=1, source_target_pairs={{0,2},{2,4},{4,6},{6,8},{8,10},{10,12},{12,14},{14,16},{16,18},{18... | collective-permute-start | bytes 1572872 | tf_op jit(solution)/shard_map/ppermute | solution.py:21
  158.4 1.3 collective-permute-start.13
  159.7 1.3 collective-permute-start.11
  161.0 1.1 slice_add_fusion.2
  162.1 0.4 pad_maximum_fusion.1
  162.5 0.2 abs_reduce_fusion.1
  162.8 1.4 copy-done.6
  164.2 0.3 round-nearest-even_convert_fusion.1
  164.5 1.3 collective-permute-start.16
  165.8 4.3 %collective-permute-done.13 = f32[2,1,1024]{2,0,1:T(2,128)S(1)} collective-permute-done((f32[2,1,1024]{2,0,1:T(2,128)S(1)}, f32[2,1,1024]{2,0,1:T(2,128)S(1)}, u32[]{:S(2)}, u32[]{:S(2)}) %collective-permute-start.13) | collective-permute-done | bytes 8224 | tf_op jit(solution)/shard_map/ppermute | solution.py:21
  170.1 14.7 %collective-permute-start.18 = (s16[2,128,1024]{2,1,0:T(8,128)(2,1)S(1)}, s16[2,128,1024]{2,1,0:T(8,128)(2,1)S(1)}, u32[]{:S(2)}, u32[]{:S(2)}) collective-permute-start(s16[2,128,1024]{2,1,0:T(8,128)(2,1)S(1)} %get-tuple-element.29), channel_id=1, source_target_pairs={{0,2},{2,4},{4,6},{6,8},{8,10},{10,12},{12,14},{14,16},{16,18},{18... | collective-permute-start | bytes 1572872 | tf_op jit(solution)/shard_map/ppermute | solution.py:21
  184.9 109.3 %all-reduce.2.cloned.1.call-done = f32[2,256,256]{2,1,0:T(8,128)} async-done(((f32[2,256,256]{2,1,0:T(8,128)}), f32[2,256,256]{2,1,0:T(8,128)}) %all-reduce.2.cloned.1.call-update) | async-done | bytes 524304 | tf_op jit(solution)/shard_map/psum | solution.py:274
  294.2 1.9 broadcast_multiply_fusion
  296.1 1.3 collective-permute-start.17
  297.4 4.5 %collective-permute-start.19 = (f32[2,1,1024]{2,0,1:T(2,128)S(1)}, f32[2,1,1024]{2,0,1:T(2,128)S(1)}, u32[]{:S(2)}, u32[]{:S(2)}) collective-permute-start(f32[2,1,1024]{2,0,1:T(2,128)S(1)} %get-tuple-element.44), channel_id=1, source_target_pairs={{0,2},{2,4},{4,6},{6,8},{8,10},{10,12},{12,14},{14,16},{16,18},{18... | collective-permute-start | bytes 24584 | tf_op jit(solution)/shard_map/ppermute | solution.py:21
  301.9 1.9 fusion.4
  303.9 1.7 fusion.2
  305.6 1.5 pad_maximum_fusion.2
  (48 shorter events, 0.3 us)
Async XLA Ops:
  7.2 78.2 %copy-start = (bf16[1,1,4,256,256]{4,3,2,1,0:T(8,128)(2,1)S(1)}, bf16[1,1,4,256,256]{4,3,2,1,0:T(8,128)(2,1)}, u32[]{:S(2)}) copy-start(bf16[1,1,4,256,256]{4,3,2,1,0:T(8,128)(2,1)} %param.12) | copy-start | bytes 1572868
  7.2 287.0 %all-reduce.2.cloned.1.call-start = ((), (), s32[]{:S(2)}) async-start(), calls=%async_computation | async-start | bytes 1048576 | tf_op jit(solution)/shard_map/psum | solution.py:274
  9.3 64.5 %collective-permute-start = (bf16[2,128,1024]{2,1,0:T(8,128)(2,1)S(1)}, bf16[2,128,1024]{2,1,0:T(8,128)(2,1)S(1)}, u32[]{:S(2)}, u32[]{:S(2)}) collective-permute-start(bf16[2,128,1024]{2,1,0:T(8,128)(2,1)S(1)} %get-tuple-element.34), channel_id=1, source_target_pairs={{0,2},{2,4},{4,6},{6,8},{8,10},{10,12},{12,14},{14,16},{16,18},{18... | collective-permute-start | bytes 1572872 | tf_op jit(solution)/shard_map/ppermute | solution.py:21
  14.2 60.4 %collective-permute-start.1 = (bf16[2,128,1024]{2,1,0:T(8,128)(2,1)S(1)}, bf16[2,128,1024]{2,1,0:T(8,128)(2,1)}, u32[]{:S(2)}, u32[]{:S(2)}) collective-permute-start(bf16[2,128,1024]{2,1,0:T(8,128)(2,1)S(1)} %get-tuple-element.34), channel_id=1, source_target_pairs={{2,0},{4,2},{6,4},{8,6},{10,8},{12,10},{14,12},{16,14},{18,16},{20... | collective-permute-start | bytes 1572872 | tf_op jit(solution)/shard_map/ppermute | solution.py:21
  63.2 9.7 %copy-start.11 = (s32[1,1,4,2]{2,3,1,0:T(2,128)S(1)}, s32[1,1,4,2]{2,3,1,0:T(2,128)}, u32[]{:S(2)}) copy-start(s32[1,1,4,2]{2,3,1,0:T(2,128)} %param.13) | copy-start | bytes 100
  72.7 12.6 %copy-start.9 = (bf16[256,256,1]{1,0,2:T(8,128)(2,1)S(1)}, bf16[256,256,1]{1,0,2:T(8,128)(2,1)}, u32[]{:S(2)}) copy-start(bf16[256,256,1]{1,0,2:T(8,128)(2,1)} %constant.26) | copy-start | bytes 393220
  73.8 0.8 copy-start.10
  76.0 15.5 %collective-permute-start.2 = (bf16[2,128,1024]{2,1,0:T(8,128)(2,1)}, bf16[2,128,1024]{2,1,0:T(8,128)(2,1)}, u32[]{:S(2)}, u32[]{:S(2)}) collective-permute-start(bf16[2,128,1024]{2,1,0:T(8,128)(2,1)} %get-tuple-element.10), channel_id=1, source_target_pairs={{0,2},{2,4},{4,6},{6,8},{8,10},{10,12},{12,14},{14,16},{16,18},{18... | collective-permute-start | bytes 1572872 | tf_op jit(solution)/shard_map/ppermute | solution.py:21
  82.1 5.4 %collective-permute-start.6 = (bf16[2,384,128]{2,1,0:T(8,128)(2,1)}, bf16[2,384,128]{2,1,0:T(8,128)(2,1)}, u32[]{:S(2)}, u32[]{:S(2)}) collective-permute-start(bf16[2,384,128]{2,1,0:T(8,128)(2,1)} %get-tuple-element.30), channel_id=1, source_target_pairs={{0,1},{2,3},{4,5},{6,7},{8,9},{10,11},{12,13},{14,15},{16,17},{18,... | collective-permute-start | bytes 589832 | tf_op jit(solution)/shard_map/ppermute | solution.py:21
  84.0 3.5 %collective-permute-start.7 = (bf16[2,384,128]{2,1,0:T(8,128)(2,1)S(1)}, bf16[2,384,128]{2,1,0:T(8,128)(2,1)}, u32[]{:S(2)}, u32[]{:S(2)}) collective-permute-start(bf16[2,384,128]{2,1,0:T(8,128)(2,1)S(1)} %get-tuple-element.31), channel_id=1, source_target_pairs={{1,0},{3,2},{5,4},{7,6},{9,8},{11,10},{13,12},{15,14},{17,16},{19,... | collective-permute-start | bytes 589832 | tf_op jit(solution)/shard_map/ppermute | solution.py:21
  85.8 22.3 %copy-start.2 = (f32[2,256,256]{2,1,0:T(8,128)S(1)}, f32[2,256,256]{2,1,0:T(8,128)}, u32[]{:S(2)}) copy-start(f32[2,256,256]{2,1,0:T(8,128)} %probe.3) | copy-start | bytes 1572868
  85.8 22.3 %copy-start.3 = (bf16[4,256,768]{2,1,0:T(8,128)(2,1)S(1)}, bf16[4,256,768]{2,1,0:T(8,128)(2,1)}, u32[]{:S(2)}) copy-start(bf16[4,256,768]{2,1,0:T(8,128)(2,1)} %constant.20.clone.left) | copy-start | bytes 4718596
  85.9 22.3 %copy-start.4 = (bf16[4,768,256]{2,1,0:T(8,128)(2,1)S(1)}, bf16[4,768,256]{2,1,0:T(8,128)(2,1)}, u32[]{:S(2)}) copy-start(bf16[4,768,256]{2,1,0:T(8,128)(2,1)} %constant.21.clone.right) | copy-start | bytes 4718596
  85.9 19.5 %collective-permute-start.3 = (bf16[2,128,1024]{2,1,0:T(8,128)(2,1)}, bf16[2,128,1024]{2,1,0:T(8,128)(2,1)S(1)}, u32[]{:S(2)}, u32[]{:S(2)}) collective-permute-start(bf16[2,128,1024]{2,1,0:T(8,128)(2,1)} %get-tuple-element.10), channel_id=1, source_target_pairs={{2,0},{4,2},{6,4},{8,6},{10,8},{12,10},{14,12},{16,14},{18,16},{20... | collective-permute-start | bytes 1572872 | tf_op jit(solution)/shard_map/ppermute | solution.py:21
  105.5 7.5 %collective-permute-start.4 = (bf16[2,384,128]{2,1,0:T(8,128)(2,1)S(1)}, bf16[2,384,128]{2,1,0:T(8,128)(2,1)S(1)}, u32[]{:S(2)}, u32[]{:S(2)}) collective-permute-start(bf16[2,384,128]{2,1,0:T(8,128)(2,1)S(1)} %get-tuple-element.32), channel_id=1, source_target_pairs={{0,1},{2,3},{4,5},{6,7},{8,9},{10,11},{12,13},{14,15},{16,17},{18,... | collective-permute-start | bytes 589832 | tf_op jit(solution)/shard_map/ppermute | solution.py:21
  106.8 6.2 %collective-permute-start.5 = (bf16[2,384,128]{2,1,0:T(8,128)(2,1)S(1)}, bf16[2,384,128]{2,1,0:T(8,128)(2,1)S(1)}, u32[]{:S(2)}, u32[]{:S(2)}) collective-permute-start(bf16[2,384,128]{2,1,0:T(8,128)(2,1)S(1)} %get-tuple-element.33), channel_id=1, source_target_pairs={{1,0},{3,2},{5,4},{7,6},{9,8},{11,10},{13,12},{15,14},{17,16},{19,... | collective-permute-start | bytes 589832 | tf_op jit(solution)/shard_map/ppermute | solution.py:21
  120.2 16.7 %copy-start.8 = (f32[2,384,1280]{2,1,0:T(8,128)S(1)}, f32[2,384,1280]{2,1,0:T(8,128)}, u32[]{:S(2)}) copy-start(f32[2,384,1280]{2,1,0:T(8,128)} %get-tuple-element.16) | copy-start | bytes 11796484
  127.4 11.5 %collective-permute-start.8 = (f32[2,384,128]{2,1,0:T(8,128)S(1)}, f32[2,384,128]{2,1,0:T(8,128)S(1)}, u32[]{:S(2)}, u32[]{:S(2)}) collective-permute-start(f32[2,384,128]{2,1,0:T(8,128)S(1)} %slice.81), channel_id=1, source_target_pairs={{0,1},{2,3},{4,5},{6,7},{8,9},{10,11},{12,13},{14,15},{16,17},{18,... | collective-permute-start | bytes 1179656 | tf_op jit(solution)/shard_map/ppermute | solution.py:21
  136.9 8.7 %collective-permute-start.14 = (f32[2,384,128]{2,1,0:T(8,128)S(1)}, f32[2,384,128]{2,1,0:T(8,128)}, u32[]{:S(2)}, u32[]{:S(2)}) collective-permute-start(f32[2,384,128]{2,1,0:T(8,128)S(1)} %slice.89), channel_id=1, source_target_pairs={{0,1},{2,3},{4,5},{6,7},{8,9},{10,11},{12,13},{14,15},{16,17},{18,... | collective-permute-start | bytes 1179656 | tf_op jit(solution)/shard_map/ppermute | solution.py:21
  140.9 7.5 %collective-permute-start.9 = (f32[2,384,128]{2,1,0:T(8,128)}, f32[2,384,128]{2,1,0:T(8,128)}, u32[]{:S(2)}, u32[]{:S(2)}) collective-permute-start(f32[2,384,128]{2,1,0:T(8,128)} %get-tuple-element.23), channel_id=1, source_target_pairs={{1,0},{3,2},{5,4},{7,6},{9,8},{11,10},{13,12},{15,14},{17,16},{19,... | collective-permute-start | bytes 1179656 | tf_op jit(solution)/shard_map/ppermute | solution.py:21
  145.6 4.0 %copy-start.7 = (f32[2,384,768]{2,1,0:T(8,128)S(1)}, f32[2,384,768]{2,1,0:T(8,128)}, u32[]{:S(2)}) copy-start(f32[2,384,768]{2,1,0:T(8,128)} %slice.82) | copy-start | bytes 7077892
  147.1 13.9 %collective-permute-start.15 = (f32[2,384,128]{2,1,0:T(8,128)S(1)}, f32[2,384,128]{2,1,0:T(8,128)S(1)}, u32[]{:S(2)}, u32[]{:S(2)}) collective-permute-start(f32[2,384,128]{2,1,0:T(8,128)S(1)} %get-tuple-element.25), channel_id=1, source_target_pairs={{1,0},{3,2},{5,4},{7,6},{9,8},{11,10},{13,12},{15,14},{17,16},{19,... | collective-permute-start | bytes 1179656 | tf_op jit(solution)/shard_map/ppermute | solution.py:21
  149.9 12.2 %copy-start.5 = (f32[2,384,1024]{2,1,0:T(8,128)}, f32[2,384,1024]{2,1,0:T(8,128)S(1)}, u32[]{:S(2)}) copy-start(f32[2,384,1024]{2,1,0:T(8,128)S(1)} %pad_maximum_fusion) | copy-start | bytes 9437188
  151.7 145.6 %collective-permute-start.10 = (s16[2,128,1024]{2,1,0:T(8,128)(2,1)}, s16[2,128,1024]{2,1,0:T(8,128)(2,1)}, u32[]{:S(2)}, u32[]{:S(2)}) collective-permute-start(s16[2,128,1024]{2,1,0:T(8,128)(2,1)} %get-tuple-element.26), channel_id=1, source_target_pairs={{2,0},{4,2},{6,4},{8,6},{10,8},{12,10},{14,12},{16,14},{18,16},{20... | collective-permute-start | bytes 1572872 | tf_op jit(solution)/shard_map/ppermute | solution.py:21
  153.0 148.9 %collective-permute-start.12 = (s16[2,128,1024]{2,1,0:T(8,128)(2,1)S(1)}, s16[2,128,1024]{2,1,0:T(8,128)(2,1)}, u32[]{:S(2)}, u32[]{:S(2)}) collective-permute-start(s16[2,128,1024]{2,1,0:T(8,128)(2,1)S(1)} %get-tuple-element.27), channel_id=1, source_target_pairs={{0,2},{2,4},{4,6},{6,8},{8,10},{10,12},{12,14},{14,16},{16,18},{18... | collective-permute-start | bytes 1572872 | tf_op jit(solution)/shard_map/ppermute | solution.py:21
  158.4 11.7 %collective-permute-start.13 = (f32[2,1,1024]{2,0,1:T(2,128)S(1)}, f32[2,1,1024]{2,0,1:T(2,128)S(1)}, u32[]{:S(2)}, u32[]{:S(2)}) collective-permute-start(f32[2,1,1024]{2,0,1:T(2,128)S(1)} %get-tuple-element.40), channel_id=1, source_target_pairs={{0,2},{2,4},{4,6},{6,8},{8,10},{10,12},{12,14},{14,16},{16,18},{18... | collective-permute-start | bytes 24584 | tf_op jit(solution)/shard_map/ppermute | solution.py:21
  159.7 136.3 %collective-permute-start.11 = (f32[2,1,1024]{2,0,1:T(2,128)S(1)}, f32[2,1,1024]{2,0,1:T(2,128)S(1)}, u32[]{:S(2)}, u32[]{:S(2)}) collective-permute-start(f32[2,1,1024]{2,0,1:T(2,128)S(1)} %get-tuple-element.38), channel_id=1, source_target_pairs={{2,0},{4,2},{6,4},{8,6},{10,8},{12,10},{14,12},{16,14},{18,16},{20... | collective-permute-start | bytes 24584 | tf_op jit(solution)/shard_map/ppermute | solution.py:21
  162.5 1.6 copy-start.6
  164.5 139.4 %collective-permute-start.16 = (s16[2,128,1024]{2,1,0:T(8,128)(2,1)S(1)}, s16[2,128,1024]{2,1,0:T(8,128)(2,1)S(1)}, u32[]{:S(2)}, u32[]{:S(2)}) collective-permute-start(s16[2,128,1024]{2,1,0:T(8,128)(2,1)S(1)} %get-tuple-element.28), channel_id=1, source_target_pairs={{2,0},{4,2},{6,4},{8,6},{10,8},{12,10},{14,12},{16,14},{18,16},{20... | collective-permute-start | bytes 1572872 | tf_op jit(solution)/shard_map/ppermute | solution.py:21
  170.1 133.8 %collective-permute-start.18 = (s16[2,128,1024]{2,1,0:T(8,128)(2,1)S(1)}, s16[2,128,1024]{2,1,0:T(8,128)(2,1)S(1)}, u32[]{:S(2)}, u32[]{:S(2)}) collective-permute-start(s16[2,128,1024]{2,1,0:T(8,128)(2,1)S(1)} %get-tuple-element.29), channel_id=1, source_target_pairs={{0,2},{2,4},{4,6},{6,8},{8,10},{10,12},{12,14},{14,16},{16,18},{18... | collective-permute-start | bytes 1572872 | tf_op jit(solution)/shard_map/ppermute | solution.py:21
  296.1 7.8 %collective-permute-start.17 = (f32[2,1,1024]{2,0,1:T(2,128)S(1)}, f32[2,1,1024]{2,0,1:T(2,128)S(1)}, u32[]{:S(2)}, u32[]{:S(2)}) collective-permute-start(f32[2,1,1024]{2,0,1:T(2,128)S(1)} %get-tuple-element.42), channel_id=1, source_target_pairs={{2,0},{4,2},{6,4},{8,6},{10,8},{12,10},{14,12},{16,14},{18,16},{20... | collective-permute-start | bytes 24584 | tf_op jit(solution)/shard_map/ppermute | solution.py:21
  297.4 6.5 %collective-permute-start.19 = (f32[2,1,1024]{2,0,1:T(2,128)S(1)}, f32[2,1,1024]{2,0,1:T(2,128)S(1)}, u32[]{:S(2)}, u32[]{:S(2)}) collective-permute-start(f32[2,1,1024]{2,0,1:T(2,128)S(1)} %get-tuple-element.44), channel_id=1, source_target_pairs={{0,2},{2,4},{4,6},{6,8},{8,10},{10,12},{12,14},{14,16},{16,18},{18... | collective-permute-start | bytes 24584 | tf_op jit(solution)/shard_map/ppermute | solution.py:21
  303.9 3.2 %copy-start.1 = (bf16[1,1,4,256,256]{4,3,2,1,0:T(8,128)(2,1)S(1)}, bf16[1,1,4,256,256]{4,3,2,1,0:T(8,128)(2,1)}, u32[]{:S(2)}) copy-start(bf16[1,1,4,256,256]{4,3,2,1,0:T(8,128)(2,1)} %param.12) | copy-start | bytes 1572868
Sparse Core Ops, SparseCore 0:
  145.7 148.3 all-reduce.1
